TPU v7x, 256 devices: a whole 4x4x8 slice. The times are simulated.
256 devices in a mesh: sect: 4 (over x), node: 64 (over z, y, core).
Axes of the slice: x: 4, y: 4, z: 8, core: 2. Of those that a mesh axis runs over, the one named last changes fastest.
Arguments:
- grid_feat: bfloat16 [65536, 512], P(('sect', 'node')), may hold values from -6 to 6
- edge_len: float32 [65536, 2], P(('sect', 'node')), may hold values from 0.2 to 1.5
- g2m_owner: int32 [65536, 2], P(('sect', 'node')), may hold values from 0 to 63, all different within a row; in each aligned block of 256 rows (0 to 255, 256 to 511, ...) at most 16 rows name the same one
- g2m_dst: int32 [65536, 2], P(('sect', 'node')), may hold values from 0 to 511
- enc_weight: bfloat16 [512, 512], replicated, may hold values from -0.25 to 0.25
- enc_vec: float32 [512], replicated, may hold values from -5 to 5
- mesh_init: bfloat16 [64, 512, 512], P('node', 'sect'), may hold values from -1.11 to 1.11
- mesh_weight: bfloat16 [512, 512], replicated, may hold values from -0.015625 to 0.015625
- halo_send: int32 [4, 64, 4, 64, 2], P('sect', 'node'), may hold values from 0 to 127
- mesh_src: int32 [64, 512, 8], P('node', 'sect'), may hold values from 0 to 639
- proc_weight: bfloat16 [2, 4, 512, 512], replicated, may hold values from -0.25 to 0.25
- cot: bfloat16 [64, 512, 512], P('node', 'sect'), may hold values from -16 to 16
Outputs:
- mesh_out: bfloat16 [64, 512, 512], P('node', 'sect')
- grid_grad: bfloat16 [65536, 512], P(('sect', 'node'))
Inputs may be any that keep to these rules, and one draw needn't show every extreme that they name: `g2m_owner`: within the 256 grid nodes of one device (aligned blocks), at most 16 edges name one mesh block, and some block is named by exactly 16 edges in some or all devices; the 2 edges of one grid node name different blocks. `mesh_src`: entries below 128 name own rows of the table, the others received rows.
All inputs are finite; a program needn't handle non-finite values.
Results may differ from a plain program's by a relative error of at most 0.009.
Values may be sent and summed in bfloat16 or wider, within the bound.
A program may use at most 64 MiB of HBM per device.

v0:
```python
import jax
import jax.numpy as jnp
from jax import lax
from jax.sharding import PartitionSpec as P

HIGH = lax.Precision.HIGHEST


def swish_slope(value):
    sig = jax.nn.sigmoid(value)
    return sig * (1.0 + value * (1.0 - sig))


def layer_norm(value):
    mean = jnp.mean(value, axis=-1, keepdims=True)
    centred = value - mean
    var = jnp.mean(centred * centred, axis=-1, keepdims=True)
    return centred * lax.rsqrt(var + 1e-05)


def node_update(value):
    return jax.nn.silu(layer_norm(value))


def back_dot(grad, weight):
    return jnp.dot(grad, weight.astype(jnp.float32).T, precision=HIGH)


def body(
    grid_feat,
    edge_len,
    g2m_owner,
    g2m_dst,
    enc_weight,
    enc_vec,
    mesh_init,
    mesh_weight,
    halo_send,
    mesh_src,
    proc_weight,
    cot,
):
    nodes = lax.axis_size("node")
    sects = lax.axis_size("sect")
    width = grid_feat.shape[1]
    grid_rows, fanout = edge_len.shape
    edges = grid_rows * fanout
    capacity = max(2, 2 * edges // nodes)
    block = mesh_init.shape[1]
    whole_block = block * sects
    pre = jnp.dot(grid_feat, enc_weight, preferred_element_type=jnp.float32)
    act = pre[:, None, :] + edge_len[:, :, None] * enc_vec
    message = jax.nn.silu(act).astype(jnp.bfloat16).reshape(edges, width)
    owner = g2m_owner.reshape(edges)
    onehot = (owner[:, None] == jnp.arange(nodes, dtype=jnp.int32)[None, :]).astype(jnp.int32)
    rank = jnp.sum((jnp.cumsum(onehot, axis=0) - 1) * onehot, axis=1)
    place = owner * capacity + rank
    send_rows = jnp.zeros((nodes * capacity, width), jnp.bfloat16).at[place].set(message)
    send_dst = jnp.zeros((nodes * capacity,), jnp.int32).at[place].set(g2m_dst.reshape(edges))
    got_rows, got_dst = (
        lax.all_to_all(
            send_rows.reshape(nodes, capacity, width),
            "node",
            split_axis=0,
            concat_axis=0,
            tiled=True,
        ),
        lax.all_to_all(
            send_dst.reshape(nodes, capacity), "node", split_axis=0, concat_axis=0, tiled=True
        ),
    )
    flat_dst = got_dst.reshape(nodes * capacity)
    partial_value = jax.ops.segment_sum(
        got_rows.reshape(nodes * capacity, width).astype(jnp.float32),
        flat_dst,
        num_segments=whole_block,
    )
    summed = lax.psum(partial_value, "sect")
    gathered = lax.dynamic_slice_in_dim(summed, lax.axis_index("sect") * block, block, 0)
    agg_low = gathered.astype(jnp.bfloat16)
    mesh_pre = jnp.dot(agg_low, mesh_weight, preferred_element_type=jnp.float32)
    state = (mesh_init[0].astype(jnp.float32) + jax.nn.silu(mesh_pre)).astype(jnp.bfloat16)
    sends = halo_send[0, 0]
    sources = mesh_src[0]
    table_len = block + sects * nodes * sends.shape[2]
    layers = proc_weight.shape[0]
    saved = []
    for layer in range(layers):
        weights = proc_weight[layer]
        incoming = lax.all_to_all(
            lax.all_to_all(state[sends], "sect", split_axis=0, concat_axis=0, tiled=True),
            "node",
            split_axis=1,
            concat_axis=1,
            tiled=True,
        )
        table = jnp.concatenate([state, incoming.reshape(-1, width)], axis=0)
        from_src = jnp.dot(table, weights[0], preferred_element_type=jnp.float32)
        to_dst = jnp.dot(state, weights[1], preferred_element_type=jnp.float32)
        joined = from_src[sources] + to_dst[:, None, :]
        agg = jnp.sum(jax.nn.silu(joined), axis=1).astype(jnp.bfloat16)
        mixed = jnp.dot(state, weights[2], preferred_element_type=jnp.float32) + jnp.dot(
            agg, weights[3], preferred_element_type=jnp.float32
        )
        saved.append((joined, mixed))
        state = (state.astype(jnp.float32) + node_update(mixed)).astype(jnp.bfloat16)
    grad = cot[0].astype(jnp.float32)
    for layer in reversed(range(layers)):
        weights = proc_weight[layer]
        joined, mixed = saved[layer]
        _, pull = jax.vjp(node_update, mixed)
        grad_mixed = pull(grad)[0]
        grad_state = grad + back_dot(grad_mixed, weights[2])
        grad_agg = back_dot(grad_mixed, weights[3])
        grad_joined = grad_agg[:, None, :] * swish_slope(joined)
        grad_state = grad_state + back_dot(jnp.sum(grad_joined, axis=1), weights[1])
        grad_src = jax.ops.segment_sum(
            grad_joined.reshape(-1, width), sources.reshape(-1), num_segments=table_len
        )
        grad_table = back_dot(grad_src, weights[0])
        returned = lax.all_to_all(
            lax.all_to_all(
                grad_table[block:].reshape(sects, nodes, -1, width),
                "sect",
                split_axis=0,
                concat_axis=0,
                tiled=True,
            ),
            "node",
            split_axis=1,
            concat_axis=1,
            tiled=True,
        )
        grad_own = jax.ops.segment_sum(
            returned.reshape(-1, width), sends.reshape(-1), num_segments=block
        )
        grad = grad_state + grad_table[:block] + grad_own
    grad_mesh_pre = grad * swish_slope(mesh_pre)
    grad_gathered = back_dot(grad_mesh_pre, mesh_weight)
    grad_partial = lax.all_gather(grad_gathered, "sect", axis=0, tiled=True)
    grad_slots = grad_partial[flat_dst].reshape(nodes, capacity, width)
    grad_back = lax.all_to_all(grad_slots, "node", split_axis=0, concat_axis=0, tiled=True)
    grad_message = grad_back.reshape(nodes * capacity, width)[place].reshape(
        grid_rows, fanout, width
    )
    grad_pre = jnp.sum(grad_message * swish_slope(act), axis=1)
    grid_grad = back_dot(grad_pre, enc_weight).astype(jnp.bfloat16)
    return (state[None], grid_grad)


def solution(mesh):
    return jax.shard_map(
        body,
        mesh=mesh,
        in_specs=(
            P(("sect", "node"), None),
            P(("sect", "node"), None),
            P(("sect", "node"), None),
            P(("sect", "node"), None),
            P(),
            P(),
            P("node", "sect", None),
            P(),
            P("sect", "node", None, None, None),
            P("node", "sect", None),
            P(),
            P("node", "sect", None),
        ),
        out_specs=(P("node", "sect", None), P(("sect", "node"), None)),
        check_vma=False,
    )
```

profile of v0, /device:TPU:8, one launch (start us, length us, event | category | flops | bytes accessed | tf_op | source)
XLA Modules:
  0.0 482.5 jit_solution(8604897864245823764)
XLA Ops:
  15.1 12.1 %all-to-all-start = ((s32[64,1,16]{2,1,0:T(1,128)}), s32[64,1,16]{2,1,0:T(1,128)S(1)}, u32[]{:S(2)}, u32[]{:S(2)}) async-start(s32[64,1,16]{2,1,0:T(1,128)} %bitcast.4), calls=%async_computation | async-start | bytes 65536 | tf_op jit(solution)/shard_map/all_to_all | solution.py:68
  29.9 3.8 scatter_custom_fusion.1
  35.7 8.3 %all-to-all-start.1 = ((bf16[64,16,512]{2,1,0:T(8,128)(2,1)}), bf16[64,16,512]{2,1,0:T(8,128)(2,1)S(1)}, u32[]{:S(2)}, u32[]{:S(2)}) async-start(bf16[64,16,512]{2,1,0:T(8,128)(2,1)} %bitcast.179), calls=%async_computation.1 | async-start | bytes 2097152 | tf_op jit(solution)/shard_map/all_to_all | solution.py:61
  45.6 27.2 %all-to-all-done.1 = bf16[64,16,512]{2,1,0:T(8,128)(2,1)S(1)} async-done(((bf16[64,16,512]{2,1,0:T(8,128)(2,1)}), bf16[64,16,512]{2,1,0:T(8,128)(2,1)S(1)}, u32[]{:S(2)}, u32[]{:S(2)}) %all-to-all-start.1) | async-done | bytes 1048608 | tf_op jit(solution)/shard_map/all_to_all | solution.py:61
  72.8 7.0 %scatter_custom_fusion.2 = f32[512,512]{1,0:T(8,128)S(1)} fusion(s32[1024]{0:T(1024)S(1)} %reshape.349, bf16[1024,512]{1,0:T(8,128)(2,1)S(1)} %bitcast.178, f32[]{:T(128)} %constant.22.clone.1), kind=kCustom, calls=%fused_computation.13 | custom fusion | flops 1048576 | bytes 2097156 | tf_op jit(solution)/shard_map/scatter-add | solution.py:73
  79.8 33.0 %all-reduce.1 = bf16[512,512]{1,0:T(8,128)(2,1)S(1)} all-reduce(f32[512,512]{1,0:T(8,128)S(1)} %scatter_custom_fusion.2), channel_id=1, replica_groups=mesh['sect'=4,'node'=64] {'sect'}, use_global_device_ids=true, to_apply=%region_6.7 | all-reduce | flops 262144 | bytes 1572864 | tf_op jit(solution)/shard_map/psum | solution.py:78
  116.9 10.6 %all_to_all.59 = bf16[4,64,2,512]{3,2,1,0:T(2,128)(2,1)S(1)} all-to-all(bf16[4,64,2,512]{3,2,1,0:T(2,128)(2,1)S(1)} %reshape.284), channel_id=1, replica_groups=mesh['sect'=4,'node'=64] {'sect'}, dimensions={0} | all-to-all | bytes 1048576 | tf_op jit(solution)/shard_map/all_to_all | solution.py:91
  128.7 6.1 %all-to-all-start.3 = ((bf16[4,64,2,512]{3,2,0,1:T(2,128)(2,1)}), bf16[4,64,2,512]{3,2,0,1:T(2,128)(2,1)S(1)}, u32[]{:S(2)}, u32[]{:S(2)}) async-start(bf16[4,64,2,512]{3,2,0,1:T(2,128)(2,1)} %copy.112), calls=%async_computation.3 | async-start | bytes 1048576 | tf_op jit(solution)/shard_map/all_to_all | solution.py:90
  138.3 14.0 %all-to-all-done.3 = bf16[4,64,2,512]{3,2,0,1:T(2,128)(2,1)S(1)} async-done(((bf16[4,64,2,512]{3,2,0,1:T(2,128)(2,1)}), bf16[4,64,2,512]{3,2,0,1:T(2,128)(2,1)S(1)}, u32[]{:S(2)}, u32[]{:S(2)}) %all-to-all-start.3) | async-done | bytes 524320 | tf_op jit(solution)/shard_map/all_to_all | solution.py:90
  154.5 4.9 %gather_fusion.1 = f32[1024,512]{1,0:T(8,128)} fusion(f32[640,512]{1,0:T(8,128)S(1)} %fusion.33, s32[1024]{0:T(1024)S(1)} %broadcast_clamp_fusion.1), kind=kCustom, calls=%fused_computation.1 | custom fusion | bytes 4198400 | tf_op jit(solution)/shard_map/gather | solution.py:100
  159.4 3.0 multiply_reduce_fusion.3
  166.4 12.3 %all_to_all.60 = bf16[4,64,2,512]{3,2,1,0:T(2,128)(2,1)S(1)} all-to-all(bf16[4,64,2,512]{3,2,1,0:T(2,128)(2,1)S(1)} %reshape.300), channel_id=1, replica_groups=mesh['sect'=4,'node'=64] {'sect'}, dimensions={0} | all-to-all | bytes 1048576 | tf_op jit(solution)/shard_map/all_to_all | solution.py:91
  179.9 5.9 %all-to-all-start.5 = ((bf16[4,64,2,512]{3,2,0,1:T(2,128)(2,1)}), bf16[4,64,2,512]{3,2,0,1:T(2,128)(2,1)S(1)}, u32[]{:S(2)}, u32[]{:S(2)}) async-start(bf16[4,64,2,512]{3,2,0,1:T(2,128)(2,1)} %copy.115), calls=%async_computation.5 | async-start | bytes 1048576 | tf_op jit(solution)/shard_map/all_to_all | solution.py:90
  190.0 13.3 %all-to-all-done.5 = bf16[4,64,2,512]{3,2,0,1:T(2,128)(2,1)S(1)} async-done(((bf16[4,64,2,512]{3,2,0,1:T(2,128)(2,1)}), bf16[4,64,2,512]{3,2,0,1:T(2,128)(2,1)S(1)}, u32[]{:S(2)}, u32[]{:S(2)}) %all-to-all-start.5) | async-done | bytes 524320 | tf_op jit(solution)/shard_map/all_to_all | solution.py:90
  206.3 4.9 %gather_fusion.3 = f32[1024,512]{1,0:T(8,128)} fusion(f32[640,512]{1,0:T(8,128)S(1)} %fusion.37, s32[1024]{0:T(1024)S(1)} %broadcast_clamp_fusion.1), kind=kCustom, calls=%fused_computation.3 | custom fusion | bytes 4198400 | tf_op jit(solution)/shard_map/gather | solution.py:100
  211.3 3.0 multiply_reduce_fusion.2
  219.8 8.8 %scatter_custom_fusion.3 = f32[640,512]{1,0:T(8,128)} fusion(s32[1024]{0:T(1024)} %reshape.357, f32[1024,512]{1,0:T(8,128)S(1)} %copy-done.2, f32[]{:T(128)} %constant.30.clone.1, f32[128,512]{1,0:T(8,128)S(1)} %fusion.44, f32[128,512]{1,0:T(8,128)} %copy-done.7, f32[]{:T(128)} %constant.22.clone.1), kind=kCustom, calls=%fused_computation.33 | custom fusion | flops 5242880 | bytes 3933184 | tf_op jit(solution)/shard_map/scatter-add | solution.py:117
  233.4 2.8 reshape.273
  236.2 19.0 %all_to_all.61 = f32[4,64,2,512]{3,2,1,0:T(2,128)S(1)} all-to-all(f32[4,64,2,512]{3,2,1,0:T(2,128)} %reshape.273), channel_id=1, replica_groups=mesh['sect'=4,'node'=64] {'sect'}, dimensions={0} | all-to-all | bytes 2097152 | tf_op jit(solution)/shard_map/all_to_all | solution.py:122
  256.9 6.5 %all-to-all-start.7 = ((f32[4,64,2,512]{3,2,0,1:T(2,128)}), f32[4,64,2,512]{3,2,0,1:T(2,128)}, u32[]{:S(2)}, u32[]{:S(2)}) async-start(f32[4,64,2,512]{3,2,0,1:T(2,128)} %copy.119), calls=%async_computation.7 | async-start | bytes 2097152 | tf_op jit(solution)/shard_map/all_to_all | solution.py:121
  271.0 20.9 %all-to-all-done.7 = f32[4,64,2,512]{3,2,0,1:T(2,128)} async-done(((f32[4,64,2,512]{3,2,0,1:T(2,128)}), f32[4,64,2,512]{3,2,0,1:T(2,128)}, u32[]{:S(2)}, u32[]{:S(2)}) %all-to-all-start.7) | async-done | bytes 1048608 | tf_op jit(solution)/shard_map/all_to_all | solution.py:121
  294.3 3.7 scatter_fusion
  301.1 8.7 %scatter_custom_fusion.5 = f32[640,512]{1,0:T(8,128)} fusion(s32[1024]{0:T(1024)} %reshape.357, f32[1024,512]{1,0:T(8,128)S(1)} %copy-done.1, f32[128,512]{1,0:T(8,128)S(1)} %fusion.56, f32[]{:T(128)} %constant.30.clone.1, f32[128,512]{1,0:T(8,128)S(1)} %fusion.60, f32[]{:T(128)} %constant.22.clone.1), kind=kCustom, calls=%fused_computation.23 | custom fusion | flops 5242880 | bytes 3933184 | tf_op jit(solution)/shard_map/scatter-add | solution.py:117
  314.5 2.8 reshape.275
  317.3 17.9 %all_to_all.62 = f32[4,64,2,512]{3,2,1,0:T(2,128)S(1)} all-to-all(f32[4,64,2,512]{3,2,1,0:T(2,128)} %reshape.275), channel_id=1, replica_groups=mesh['sect'=4,'node'=64] {'sect'}, dimensions={0} | all-to-all | bytes 2097152 | tf_op jit(solution)/shard_map/all_to_all | solution.py:122
  336.8 6.8 %all-to-all-start.9 = ((f32[4,64,2,512]{3,2,0,1:T(2,128)}), f32[4,64,2,512]{3,2,0,1:T(2,128)}, u32[]{:S(2)}, u32[]{:S(2)}) async-start(f32[4,64,2,512]{3,2,0,1:T(2,128)} %copy.121), calls=%async_computation.9 | async-start | bytes 2097152 | tf_op jit(solution)/shard_map/all_to_all | solution.py:121
  349.4 23.0 %all-to-all-done.9 = f32[4,64,2,512]{3,2,0,1:T(2,128)} async-done(((f32[4,64,2,512]{3,2,0,1:T(2,128)}), f32[4,64,2,512]{3,2,0,1:T(2,128)}, u32[]{:S(2)}, u32[]{:S(2)}) %all-to-all-start.9) | async-done | bytes 1048608 | tf_op jit(solution)/shard_map/all_to_all | solution.py:121
  374.7 3.7 scatter_fusion.1
  379.9 21.1 %all-gather.2.cloned.1.call-done = f32[512,512]{1,0:T(8,128)} async-done(((f32[128,512]{1,0:T(8,128)}), f32[512,512]{1,0:T(8,128)}) %all-gather.2.cloned.1.call-update) | async-done | bytes 1048592 | tf_op jit(solution)/shard_map/all_gather | solution.py:140
  401.0 6.5 %gather_fusion.4 = f32[1024,512]{1,0:T(8,128)} fusion(f32[512,512]{1,0:T(8,128)} %all-gather.2.cloned.1.call-done, s32[1024]{0:T(1024)S(1)} %broadcast_clamp_fusion), kind=kCustom, calls=%fused_computation.4 | custom fusion | bytes 4198400 | tf_op jit(solution)/shard_map/gather | solution.py:141
  407.5 10.6 %all-to-all-start.10 = ((f32[64,16,512]{2,1,0:T(8,128)}), f32[64,16,512]{2,1,0:T(8,128)S(1)}, u32[]{:S(2)}, u32[]{:S(2)}) async-start(f32[64,16,512]{2,1,0:T(8,128)} %bitcast.177), calls=%async_computation.10 | async-start | bytes 4194304 | tf_op jit(solution)/shard_map/all_to_all | solution.py:142
  418.1 51.3 %all-to-all-done.10 = f32[64,16,512]{2,1,0:T(8,128)S(1)} async-done(((f32[64,16,512]{2,1,0:T(8,128)}), f32[64,16,512]{2,1,0:T(8,128)S(1)}, u32[]{:S(2)}, u32[]{:S(2)}) %all-to-all-start.10) | async-done | bytes 2097184 | tf_op jit(solution)/shard_map/all_to_all | solution.py:142
  (165 shorter events, 83.9 us)
Async XLA Ops:
  7.2 20.0 %copy-start = (bf16[512,512]{1,0:T(8,128)(2,1)S(1)}, bf16[512,512]{1,0:T(8,128)(2,1)}, u32[]{:S(2)}) copy-start(bf16[512,512]{1,0:T(8,128)(2,1)} %param.16) | copy-start | bytes 1572868
  7.2 21.3 %copy-start.21 = (f32[256,2]{0,1:T(2,128)S(1)}, f32[256,2]{0,1:T(2,128)}, u32[]{:S(2)}) copy-start(f32[256,2]{0,1:T(2,128)} %param.13) | copy-start | bytes 6148
  15.1 20.6 %all-to-all-start = ((s32[64,1,16]{2,1,0:T(1,128)}), s32[64,1,16]{2,1,0:T(1,128)S(1)}, u32[]{:S(2)}, u32[]{:S(2)}) async-start(s32[64,1,16]{2,1,0:T(1,128)} %bitcast.4), calls=%async_computation | async-start | bytes 65536 | tf_op jit(solution)/shard_map/all_to_all | solution.py:68
  28.5 5.2 %copy-start.5 = (f32[256,512]{1,0:T(8,128)}, f32[256,512]{1,0:T(8,128)S(1)}, u32[]{:S(2)}) copy-start(f32[256,512]{1,0:T(8,128)S(1)} %fusion.128) | copy-start | bytes 1572868
  29.9 14.1 %copy-start.20 = (s32[1,1,4,64,2]{3,4,2,1,0:T(2,128)S(1)}, s32[1,1,4,64,2]{3,4,2,1,0:T(2,128)}, u32[]{:S(2)}) copy-start(s32[1,1,4,64,2]{3,4,2,1,0:T(2,128)} %param.20) | copy-start | bytes 6148
  35.7 44.0 %copy-start.17 = (s32[64,1,16]{2,1,0:T(1,128)}, s32[64,1,16]{2,1,0:T(1,128)S(1)}, u32[]{:S(2)}) copy-start(s32[64,1,16]{2,1,0:T(1,128)S(1)} %all-to-all-done) | copy-start | bytes 12292
  35.7 37.1 %all-to-all-start.1 = ((bf16[64,16,512]{2,1,0:T(8,128)(2,1)}), bf16[64,16,512]{2,1,0:T(8,128)(2,1)S(1)}, u32[]{:S(2)}, u32[]{:S(2)}) async-start(bf16[64,16,512]{2,1,0:T(8,128)(2,1)} %bitcast.179), calls=%async_computation.1 | async-start | bytes 2097152 | tf_op jit(solution)/shard_map/all_to_all | solution.py:61
  44.0 68.8 %copy-start.30 = (bf16[1,128,512]{2,1,0:T(8,128)(2,1)S(1)}, bf16[1,128,512]{2,1,0:T(8,128)(2,1)}, u32[]{:S(2)}) copy-start(bf16[1,128,512]{2,1,0:T(8,128)(2,1)} %param.18) | copy-start | bytes 393220
  116.7 18.1 %copy-start.19 = (s32[1,128,8]{1,2,0:T(8,128)S(1)}, s32[1,128,8]{1,2,0:T(8,128)}, u32[]{:S(2)}) copy-start(s32[1,128,8]{1,2,0:T(8,128)} %param.21) | copy-start | bytes 12292
  128.7 23.6 %all-to-all-start.3 = ((bf16[4,64,2,512]{3,2,0,1:T(2,128)(2,1)}), bf16[4,64,2,512]{3,2,0,1:T(2,128)(2,1)S(1)}, u32[]{:S(2)}, u32[]{:S(2)}) async-start(bf16[4,64,2,512]{3,2,0,1:T(2,128)(2,1)} %copy.112), calls=%async_computation.3 | async-start | bytes 1048576 | tf_op jit(solution)/shard_map/all_to_all | solution.py:90
  159.4 3.0 copy-start.16
  164.0 2.2 copy-start.27
  164.0 2.2 copy-start.25
  179.9 23.4 %all-to-all-start.5 = ((bf16[4,64,2,512]{3,2,0,1:T(2,128)(2,1)}), bf16[4,64,2,512]{3,2,0,1:T(2,128)(2,1)S(1)}, u32[]{:S(2)}, u32[]{:S(2)}) async-start(bf16[4,64,2,512]{3,2,0,1:T(2,128)(2,1)} %copy.115), calls=%async_computation.5 | async-start | bytes 1048576 | tf_op jit(solution)/shard_map/all_to_all | solution.py:90
  187.9 23.4 %copy-start.7 = (f32[128,512]{1,0:T(8,128)}, f32[128,512]{1,0:T(8,128)S(1)}, u32[]{:S(2)}) copy-start(f32[128,512]{1,0:T(8,128)S(1)} %fusion.48) | copy-start | bytes 786436
  211.3 3.1 copy-start.15
  211.3 4.8 copy-start.14
  214.3 5.4 %copy-start.2 = (f32[1024,512]{1,0:T(8,128)S(1)}, f32[1024,512]{1,0:T(8,128)}, u32[]{:S(2)}) copy-start(f32[1024,512]{1,0:T(8,128)} %gather_fusion.3) | copy-start | bytes 6291460
  219.7 11.5 %copy-start.13 = (f32[128,512]{1,0:T(8,128)}, f32[128,512]{1,0:T(8,128)S(1)}, u32[]{:S(2)}) copy-start(f32[128,512]{1,0:T(8,128)S(1)} %fusion.44) | copy-start | bytes 786436
  256.9 10.1 %copy-start.8 = (f32[128,512]{1,0:T(8,128)S(1)}, f32[128,512]{1,0:T(8,128)}, u32[]{:S(2)}) copy-start(f32[128,512]{1,0:T(8,128)} %copy-done.7) | copy-start | bytes 786436
  256.9 35.0 %all-to-all-start.7 = ((f32[4,64,2,512]{3,2,0,1:T(2,128)}), f32[4,64,2,512]{3,2,0,1:T(2,128)}, u32[]{:S(2)}, u32[]{:S(2)}) async-start(f32[4,64,2,512]{3,2,0,1:T(2,128)} %copy.119), calls=%async_computation.7 | async-start | bytes 2097152 | tf_op jit(solution)/shard_map/all_to_all | solution.py:121
  294.2 3.7 copy-start.26
  294.2 4.0 copy-start.28
  298.0 3.1 copy-start.1
  301.1 11.3 %copy-start.12 = (f32[128,512]{1,0:T(8,128)}, f32[128,512]{1,0:T(8,128)S(1)}, u32[]{:S(2)}) copy-start(f32[128,512]{1,0:T(8,128)S(1)} %fusion.56) | copy-start | bytes 786436
  335.2 8.5 %copy-start.10 = (f32[128,512]{1,0:T(8,128)S(1)}, f32[128,512]{1,0:T(8,128)}, u32[]{:S(2)}) copy-start(f32[128,512]{1,0:T(8,128)} %copy-done.9) | copy-start | bytes 786436
  336.8 35.5 %all-to-all-start.9 = ((f32[4,64,2,512]{3,2,0,1:T(2,128)}), f32[4,64,2,512]{3,2,0,1:T(2,128)}, u32[]{:S(2)}, u32[]{:S(2)}) async-start(f32[4,64,2,512]{3,2,0,1:T(2,128)} %copy.121), calls=%async_computation.9 | async-start | bytes 2097152 | tf_op jit(solution)/shard_map/all_to_all | solution.py:121
  343.7 57.4 %all-gather.2.cloned.1.call-start = ((), (), s32[]{:S(2)}) async-start(), calls=%async_computation.11 | async-start | bytes 1310720 | tf_op jit(solution)/shard_map/all_gather | solution.py:140
  374.7 3.8 copy-start.29
  374.7 3.8 copy-start.31
  374.7 5.1 %copy-start.18 = (s32[64,1,16]{2,1,0:T(1,128)S(1)}, s32[64,1,16]{2,1,0:T(1,128)}, u32[]{:S(2)}) copy-start(s32[64,1,16]{2,1,0:T(1,128)} %copy-done.17) | copy-start | bytes 12292
  407.5 61.8 %all-to-all-start.10 = ((f32[64,16,512]{2,1,0:T(8,128)}), f32[64,16,512]{2,1,0:T(8,128)S(1)}, u32[]{:S(2)}, u32[]{:S(2)}) async-start(f32[64,16,512]{2,1,0:T(8,128)} %bitcast.177), calls=%async_computation.10 | async-start | bytes 4194304 | tf_op jit(solution)/shard_map/all_to_all | solution.py:142
  (8 other events, 10.7 us)
Sparse Core Ops, SparseCore 0:
  379.9 21.0 all-gather.1
where the time goes:
time: 492 us; the launch traced here: 483 us
  waiting for transfers between devices  173 us (35%)
  blocking collectives  92.9 us (19%)
  local copies, waits for them, and re-layouts  59.1 us (12%)
  starting transfers between devices  56.3 us (11%)
  other arithmetic  52 us (11%)
  matrix products  34.3 us (7%)
  between operations  15.1 us (3%)
    all_to_all x1, waiting for transfers between devices, body(): lax.all_to_all(grad_slots, 'node', split_axis=0, concat_axis=0, tiled=True)  51.3 us
    all_to_all x2, waiting for transfers between devices, body(): lax.all_to_all(lax.all_to_all(grad_table[block:].reshape(sects, nodes, -1...  43.9 us
    all_to_all x2, blocking collectives, body(): lax.all_to_all(grad_table[block:].reshape(sects, nodes, -1, width), 'sect...  36.9 us
    psum x1, blocking collectives, body(): summed = lax.psum(partial_value, 'sect')  33 us
    all_to_all x2, waiting for transfers between devices, body(): lax.all_to_all(lax.all_to_all(state[sends], 'sect', split_axis=0, concat_...  27.3 us
    all_to_all x1, waiting for transfers between devices, body(): lax.all_to_all(send_rows.reshape(nodes, capacity, width), 'node', split_a...  27.2 us
    all_to_all x2, blocking collectives, body(): lax.all_to_all(state[sends], 'sect', split_axis=0, concat_axis=0, tiled=T...  23 us
    all_gather x1, waiting for transfers between devices, body(): grad_partial = lax.all_gather(grad_gathered, 'sect', axis=0, tiled=True)  21.1 us
  transfers between devices with their start and end apart: 8, of which 8 were waited for; matrix products, arithmetic and copies ran while one was open for 6% of the time, Pallas kernels for 0%

commit v1 on v0

v1 whole, which is shorter than its diff:
```python
import functools

import jax
import jax.numpy as jnp
from jax import lax
from jax.experimental import pallas as pl
from jax.experimental.pallas import tpu as pltpu
from jax.sharding import PartitionSpec as P

MESH = pl.DeviceIdType.MESH
F32 = jnp.float32
BF16 = jnp.bfloat16
NN = ((1,), (0,))
NT = ((1,), (1,))
TN = ((0,), (0,))
LANES = 128
CHUNKS = 2


def dot(left, right, dims=NN):
    return lax.dot_general(left, right, (dims, ((), ())), preferred_element_type=F32)


def iota(shape, dim):
    return lax.broadcasted_iota(jnp.int32, shape, dim)


def slope_of(value, sig):
    return sig * (1.0 + value * (1.0 - sig))


def fused(
    sects,
    nodes,
    feat,
    length,
    owner,
    dest,
    enc_w,
    vec,
    init,
    mesh_w,
    sends,
    sources,
    proc_w,
    cot,
    mesh_out,
    grid_grad,
    dst_out,
    dst_in,
    msg_out,
    msg_in,
    part_out,
    part_in,
    halo_out,
    halo_in,
    back_out,
    back_in,
    gath_out,
    gath_in,
    slot_out,
    slot_in,
    pick,
    scat,
    edge_pick,
    act_slope,
    joined,
    far_part,
    far_grad,
    piece,
    last_part,
    send_sem,
    recv_sem,
):
    sect = lax.axis_index("sect")
    node = lax.axis_index("node")
    world = sects * nodes
    zero = lax.div(sect, sects)
    line = sect * nodes + node
    grid_rows, fanout = length.shape
    block, degree = sources.shape
    width = feat.shape[1]
    whole = block * sects
    cap = msg_out.shape[2]
    slots = nodes * cap
    chunks = msg_out.shape[0]
    part = width // chunks
    layers = proc_w.shape[0]
    fan = halo_out.shape[2]
    halo = world * fan

    barrier = pltpu.get_barrier_semaphore()

    def greet_node(step, carry):
        peer = lax.rem(node + step, nodes)
        pl.semaphore_signal(barrier, inc=1, device_id=(sect, peer), device_id_type=MESH)
        return carry

    def greet_sect(step, carry):
        peer = lax.rem(sect + step, sects)
        pl.semaphore_signal(barrier, inc=1, device_id=(peer, node), device_id_type=MESH)
        return carry

    lax.fori_loop(1, nodes, greet_node, 0)
    lax.fori_loop(1, sects, greet_sect, 0)

    def push(src, dst, at, device):
        pltpu.make_async_remote_copy(
            src_ref=src,
            dst_ref=dst,
            send_sem=send_sem.at[at],
            recv_sem=recv_sem.at[at],
            device_id=device,
            device_id_type=MESH,
        ).start()

    def over_nodes(src, dst, at):
        def step(off, carry):
            peer = lax.rem(node + off, nodes)
            push(src.at[peer], dst.at[node], at, (sect, peer))
            return carry

        lax.fori_loop(1, nodes, step, 0, unroll=9)

    def over_all(src, dst, at):
        def step(off, carry):
            peer = lax.rem(line + off, world)
            push(
                src.at[peer],
                dst.at[line],
                at,
                (lax.div(peer, nodes), lax.rem(peer, nodes)),
            )
            return carry

        lax.fori_loop(1, world, step, 0, unroll=15)

    def landed(ref, count, sem):
        some = ref.at[pl.ds(0, count)]
        pltpu.make_async_copy(some, some, sem).wait()

    at_dst = 0
    at_msg = 1
    at_part = at_msg + chunks
    at_halo = at_part + chunks
    at_back = at_halo + layers
    at_gath = at_back + layers
    at_slot = at_gath + chunks

    upper = (iota((grid_rows, grid_rows), 0) < iota((grid_rows, grid_rows), 1)).astype(BF16)
    used = jnp.zeros((nodes, 1), F32)
    table = jnp.zeros((nodes, LANES), F32)
    for k in range(fanout):
        own_row = owner[k : k + 1, :]
        dst_row = dest[k : k + 1, :]
        hot = (iota((nodes, grid_rows), 0) == own_row).astype(F32)
        before = dot(hot.astype(BF16), upper) + used
        rank = jnp.sum(hot * before, axis=0, keepdims=True).astype(jnp.int32)
        used = used + jnp.sum(hot, axis=1, keepdims=True)
        place = own_row * cap + rank
        pick[:, k * grid_rows : (k + 1) * grid_rows] = (
            iota((slots, grid_rows), 0) == place
        ).astype(BF16)
        level = (iota((LANES, grid_rows), 0) == rank).astype(BF16)
        high = (hot * (dst_row >> 4).astype(F32)).astype(BF16)
        low = (hot * ((dst_row & 15) + 1).astype(F32)).astype(BF16)
        table = table + 16.0 * dot(high, level, NT) + dot(low, level, NT)
    dst_out[...] = table.reshape(nodes, 1, LANES)

    pre = dot(feat[...], enc_w[...])
    acts = [pre + length[:, k : k + 1] * vec[...] for k in range(fanout)]
    sigs = [jax.nn.sigmoid(act) for act in acts]
    message = jnp.concatenate(
        [(act * sig).astype(BF16) for act, sig in zip(acts, sigs)], axis=0
    )

    pl.semaphore_wait(barrier, nodes + sects - 2)
    over_nodes(dst_out, dst_in, at_dst)
    dst_in[node] = dst_out[node]
    for c in range(chunks):
        cols = slice(c * part, (c + 1) * part)
        msg_out[c] = dot(pick[...], message[:, cols]).astype(BF16).reshape(nodes, cap, part)
        over_nodes(msg_out.at[c], msg_in.at[c], at_msg + c)
        msg_in[c, node] = msg_out[c, node]

    for k in range(fanout):
        act_slope[k] = slope_of(acts[k], sigs[k])

    for k in range(degree):
        edge_pick[k * block : (k + 1) * block, :] = (
            iota((block, block + halo), 1) == sources[:, k : k + 1]
        ).astype(BF16)
    halo_pick = (iota((block, halo), 0) == sends[...]).astype(BF16)

    landed(dst_in, nodes - 1, recv_sem.at[at_dst])
    got = dst_in[...].reshape(nodes, LANES)
    got_high = jnp.floor(got * (1.0 / 16.0))
    got_low = got - 16.0 * got_high
    spread = (lax.rem(iota((LANES, slots), 1), cap) == iota((LANES, slots), 0)).astype(BF16)
    mine = (lax.div(iota((nodes, slots), 1), cap) == iota((nodes, slots), 0)).astype(F32)
    wide = 16.0 * dot(got_high.astype(BF16), spread) + dot(got_low.astype(BF16), spread)
    got_row = jnp.sum(wide * mine, axis=0, keepdims=True).astype(jnp.int32) - 1
    scat[...] = (iota((whole, slots), 0) == got_row).astype(BF16)

    mesh_pre = jnp.zeros((block, width), F32)
    own_part = []
    for c in range(chunks):
        landed(msg_in.at[c], nodes - 1, recv_sem.at[at_msg + c])
        agg = dot(scat[...], msg_in[c].reshape(slots, part))
        part_out[c] = agg.astype(BF16).reshape(sects, block, part)
        for off in range(1, sects):
            peer = lax.rem(sect + off, sects)
            push(part_out.at[c, peer], part_in.at[c, sect], at_part + c, (peer, node))
        part_in[c, sect] = part_out[c, sect]
    for c in range(chunks):
        landed(part_in.at[c], sects - 1, recv_sem.at[at_part + c])
        total = jnp.sum(part_in[c].astype(F32), axis=0)
        last_part[c, :block, :] = dot(total.astype(BF16), mesh_w[c * part : (c + 1) * part, :])
    for c in range(chunks):
        mesh_pre = mesh_pre + last_part[zero + c, :block, :]
    mesh_sig = jax.nn.sigmoid(mesh_pre)
    state = (init[...].astype(F32) + mesh_pre * mesh_sig).astype(BF16)

    saved = []
    for layer in range(layers):
        out = dot(halo_pick, state, TN).astype(BF16)
        halo_out[layer] = out.reshape(world, fan, width)
        over_all(halo_out.at[layer], halo_in.at[layer], at_halo + layer)
        halo_in[layer, line] = halo_out[layer, line]
        near = dot(edge_pick[:, :block], state).astype(BF16)
        piece[2] = dot(state, proc_w[layer, 1])
        joined[layer] = dot(near, proc_w[layer, 0])
        piece[1] = dot(state, proc_w[layer, 2])
        if layer > 0:
            prev = joined[layer - 1]
            joined[layer - 1] = slope_of(prev, jax.nn.sigmoid(prev))
        landed(halo_in.at[layer], world - 1, recv_sem.at[at_halo + layer])
        far = dot(edge_pick[:, block:], halo_in[layer].reshape(halo, width)).astype(BF16)
        far_part[...] = dot(far, proc_w[layer, 0])
        agg = jnp.zeros((block, width), F32)
        to_dst = piece[zero + 2]
        for k in range(degree):
            rows = slice(k * block, (k + 1) * block)
            full = joined[zero + layer, rows, :] + far_part[rows, :] + to_dst
            joined[layer, rows, :] = full
            agg = agg + full * jax.nn.sigmoid(full)
        agg = agg.astype(BF16)
        piece[0] = dot(agg, proc_w[layer, 3])
        mixed = piece[zero + 1] + piece[zero]
        centred = mixed - jnp.mean(mixed, axis=1, keepdims=True)
        scale = lax.rsqrt(jnp.mean(centred * centred, axis=1, keepdims=True) + 1e-05)
        normed = centred * scale
        sig = jax.nn.sigmoid(normed)
        saved.append((normed, scale, slope_of(normed, sig)))
        state = (state.astype(F32) + normed * sig).astype(BF16)
    mesh_out[...] = state
    last = joined[layers - 1]
    joined[layers - 1] = slope_of(last, jax.nn.sigmoid(last))

    grad = cot[...].astype(F32)
    for layer in reversed(range(layers)):
        normed, scale, slope = saved[layer]
        grad_normed = grad * slope
        grad_mixed = scale * (
            grad_normed
            - jnp.mean(grad_normed, axis=1, keepdims=True)
            - normed * jnp.mean(grad_normed * normed, axis=1, keepdims=True)
        )
        grad_mixed = grad_mixed.astype(BF16)
        grad_agg = dot(grad_mixed, proc_w[layer, 3], NT)
        grad_dst = jnp.zeros((block, width), F32)
        for k in range(degree):
            rows = slice(k * block, (k + 1) * block)
            grad_joined = joined[layer, rows, :] * grad_agg
            grad_dst = grad_dst + grad_joined
            far_grad[rows, :] = grad_joined.astype(BF16)
        grad_dst = grad_dst.astype(BF16)
        out = dot(edge_pick[:, block:], far_grad[...], TN).astype(BF16)
        back_out[layer] = out.reshape(world, fan, width)
        over_all(back_out.at[layer], back_in.at[layer], at_back + layer)
        back_in[layer, line] = back_out[layer, line]
        piece[0] = dot(grad_mixed, proc_w[layer, 2], NT)
        piece[1] = dot(grad_dst, proc_w[layer, 1], NT)
        piece[2] = dot(edge_pick[:, :block], far_grad[...], TN)
        landed(back_in.at[layer], world - 1, recv_sem.at[at_back + layer])
        piece[3] = dot(halo_pick, back_in[layer].reshape(halo, width))
        grad_src = (piece[zero + 2] + piece[zero + 3]).astype(BF16)
        piece[4] = dot(grad_src, proc_w[layer, 0], NT)
        grad = grad + piece[zero] + piece[zero + 1] + piece[zero + 4]

    grad_pre = (grad * slope_of(mesh_pre, mesh_sig)).astype(BF16)
    for c in range(chunks):
        cols = slice(c * part, (c + 1) * part)
        gath_out[c] = dot(grad_pre, mesh_w[cols, :], NT).astype(BF16)
        for off in range(1, sects):
            peer = lax.rem(sect + off, sects)
            push(gath_out.at[c], gath_in.at[c, sect], at_gath + c, (peer, node))
        gath_in[c, sect] = gath_out[c]
    for c in range(chunks):
        landed(gath_in.at[c], sects - 1, recv_sem.at[at_gath + c])
        rows = dot(scat[...], gath_in[c].reshape(whole, part), TN).astype(BF16)
        slot_out[c] = rows.reshape(nodes, cap, part)
        over_nodes(slot_out.at[c], slot_in.at[c], at_slot + c)
        slot_in[c, node] = slot_out[c, node]
    for c in range(chunks):
        cols = slice(c * part, (c + 1) * part)
        landed(slot_in.at[c], nodes - 1, recv_sem.at[at_slot + c])
        back = dot(pick[...], slot_in[c].reshape(slots, part), TN)
        grad_act = jnp.zeros((grid_rows, part), F32)
        for k in range(fanout):
            grad_act = grad_act + (
                back[k * grid_rows : (k + 1) * grid_rows] * act_slope[k, :, cols]
            )
        last_part[c] = dot(grad_act.astype(BF16), enc_w[:, cols], NT)
    total = last_part[zero]
    for c in range(1, chunks):
        total = total + last_part[zero + c]
    grid_grad[...] = total.astype(BF16)

    landed(dst_out, nodes - 1, send_sem.at[at_dst])
    for c in range(chunks):
        landed(msg_out.at[c], nodes - 1, send_sem.at[at_msg + c])
        landed(part_out.at[c], sects - 1, send_sem.at[at_part + c])
        landed(gath_in.at[c], sects - 1, send_sem.at[at_gath + c])
        landed(slot_out.at[c], nodes - 1, send_sem.at[at_slot + c])
    for layer in range(layers):
        landed(halo_out.at[layer], world - 1, send_sem.at[at_halo + layer])
        landed(back_out.at[layer], world - 1, send_sem.at[at_back + layer])


def body(
    grid_feat,
    edge_len,
    g2m_owner,
    g2m_dst,
    enc_weight,
    enc_vec,
    mesh_init,
    mesh_weight,
    halo_send,
    mesh_src,
    proc_weight,
    cot,
):
    nodes = lax.axis_size("node")
    sects = lax.axis_size("sect")
    world = nodes * sects
    grid_rows, width = grid_feat.shape
    fanout = edge_len.shape[1]
    cap = max(2, 2 * grid_rows * fanout // nodes)
    block = mesh_init.shape[1]
    fan = halo_send.shape[4]
    layers = proc_weight.shape[0]
    degree = mesh_src.shape[2]
    slots = nodes * cap
    chunks = CHUNKS
    part = width // chunks
    whole = block * sects
    count = 1 + 4 * chunks + 2 * layers
    vmem = pl.BlockSpec(memory_space=pltpu.VMEM)
    out = pl.pallas_call(
        functools.partial(fused, sects, nodes),
        out_shape=(
            jax.ShapeDtypeStruct((block, width), BF16),
            jax.ShapeDtypeStruct((grid_rows, width), BF16),
        ),
        in_specs=[vmem] * 12,
        out_specs=(vmem, vmem),
        scratch_shapes=[
            pltpu.VMEM((nodes, 1, LANES), F32),
            pltpu.VMEM((nodes, 1, LANES), F32),
            pltpu.VMEM((chunks, nodes, cap, part), BF16),
            pltpu.VMEM((chunks, nodes, cap, part), BF16),
            pltpu.VMEM((chunks, sects, block, part), BF16),
            pltpu.VMEM((chunks, sects, block, part), BF16),
            pltpu.VMEM((layers, world, fan, width), BF16),
            pltpu.VMEM((layers, world, fan, width), BF16),
            pltpu.VMEM((layers, world, fan, width), BF16),
            pltpu.VMEM((layers, world, fan, width), BF16),
            pltpu.VMEM((chunks, block, part), BF16),
            pltpu.VMEM((chunks, sects, block, part), BF16),
            pltpu.VMEM((chunks, nodes, cap, part), BF16),
            pltpu.VMEM((chunks, nodes, cap, part), BF16),
            pltpu.VMEM((slots, fanout * grid_rows), BF16),
            pltpu.VMEM((whole, slots), BF16),
            pltpu.VMEM((degree * block, block + world * fan), BF16),
            pltpu.VMEM((fanout, grid_rows, width), F32),
            pltpu.VMEM((layers, degree * block, width), F32),
            pltpu.VMEM((degree * block, width), F32),
            pltpu.VMEM((degree * block, width), BF16),
            pltpu.VMEM((5, block, width), F32),
            pltpu.VMEM((chunks, grid_rows, width), F32),
            pltpu.SemaphoreType.DMA((count,)),
            pltpu.SemaphoreType.DMA((count,)),
        ],
        compiler_params=pltpu.CompilerParams(
            collective_id=0, has_side_effects=True, vmem_limit_bytes=60 * 2**20
        ),
        name="grid_mesh",
    )(
        grid_feat,
        edge_len,
        g2m_owner.T,
        g2m_dst.T,
        enc_weight,
        enc_vec.reshape(1, width),
        mesh_init[0],
        mesh_weight,
        halo_send.reshape(1, world * fan),
        mesh_src[0],
        proc_weight,
        cot[0],
    )
    return (out[0][None], out[1])


def solution(mesh):
    return jax.shard_map(
        body,
        mesh=mesh,
        in_specs=(
            P(("sect", "node"), None),
            P(("sect", "node"), None),
            P(("sect", "node"), None),
            P(("sect", "node"), None),
            P(),
            P(),
            P("node", "sect", None),
            P(),
            P("sect", "node", None, None, None),
            P("node", "sect", None),
            P(),
            P("node", "sect", None),
        ),
        out_specs=(P("node", "sect", None), P(("sect", "node"), None)),
        check_vma=False,
    )
```

time: 492 us -> 164 us (0.33); the launches traced: 483 us -> 162 us
  waiting for transfers between devices: 173 us -> 0 us
  Pallas kernels: 0 us -> 154 us
  blocking collectives: 92.9 us -> 0 us
  starting transfers between devices: 56.3 us -> 0 us
  other arithmetic: 52 us -> 0 us
  local copies, waits for them, and re-layouts: 59.1 us -> 7.63 us
  matrix products: 34.3 us -> 0 us
  between operations: 15.1 us -> 0.65 us
    pallas_call x0 -> x1, Pallas kernels: none -> 154 us  [body(): pl.pallas_call(functools.partial(fused, sects, nodes), out_shape=(jax.Sha...]
    all_to_all x7 -> x0, waiting for transfers between devices: 152 us -> none  [the longest x1 51.3 us: body(): lax.all_to_all(grad_slots, 'node', split_axis=0, concat_axis=0, tiled=True)]
    all_to_all x4 -> x0, blocking collectives: 59.9 us -> none  [the longest x2 36.9 us: body(): lax.all_to_all(grad_table[block:].reshape(sects, nodes, -1, width), 'sect...]
    all_to_all x7 -> x0, starting transfers between devices: 56.3 us -> none  [the longest x2 13.3 us: body(): lax.all_to_all(lax.all_to_all(grad_table[block:].reshape(sects, nodes, -1...]
    dot_general x20 -> x0, matrix products: 34.3 us -> none  [the longest x10 18.4 us: back_dot(): return jnp.dot(grad, weight.astype(jnp.float32).T, precision=HIGH)]
    psum x1 -> x0, blocking collectives: 33 us -> none  [body(): summed = lax.psum(partial_value, 'sect')]
    scatter-add x5 -> x0, other arithmetic: 31.9 us -> none  [the longest x2 17.5 us: body(): jax.ops.segment_sum(grad_joined.reshape(-1, width), sources.reshape(-1),...]
    gather x8 -> x0, local copies, waits for them, and re-layouts: 23 us -> none  [the longest x2 9.82 us: body(): joined = from_src[sources] + to_dst[:, None, :]]
  transfers between devices with their start and end apart: 8 -> 0, of which waited for: 8 -> 0; matrix products, arithmetic and copies ran while one was open for 6% -> 0% of each run, Pallas kernels for 0% -> 0%
where the time goes in v1:
time: 164 us; the launch traced here: 162 us
  Pallas kernels  154 us (94%)
  local copies, waits for them, and re-layouts  7.63 us (5%)
    pallas_call x1, Pallas kernels, body(): pl.pallas_call(functools.partial(fused, sects, nodes), out_shape=(jax.Sha...  154 us
    unnamed x5, local copies, waits for them, and re-layouts  6.92 us

profile of v1, /device:TPU:8, one launch (start us, length us, event | category | flops | bytes accessed | tf_op | source)
XLA Modules:
  0.0 162.3 jit_solution(11004648061856652094)
XLA Ops:
  0.6 1.4 copy.18
  2.0 1.5 copy.19.length
  3.5 0.8 copy.17
  4.3 0.7 reshape.11.sends
  5.0 154.0 %grid_mesh.1 = (bf16[128,512]{1,0:T(8,128)(2,1)}, bf16[256,512]{1,0:T(8,128)(2,1)}) custom-call(bf16[256,512]{1,0:T(8,128)(2,1)} %feat.1, f32[256,2]{1,0:T(8,128)} %copy.19.length, s32[2,256]{1,0:T(2,128)} %bitcast.13, s32[2,256]{1,0:T(2,128)} %bitcast.14, bf16[512,512]{1,0:T(8,128)(2,1)} %enc_w.1, f32[1,512]{1,0:T(1,128)} %bitcast.15, ...), custom_call_target="tpu_custom_call" | custom-call | tf_op jit(solution)/shard_map/grid_mesh/pallas_call | solution.py:361
  159.0 1.6 copy.22
  160.6 1.7 %copy.23 = bf16[256,512]{1,0:T(8,128)(2,1)} copy(bf16[256,512]{1,0:T(8,128)(2,1)} %get-tuple-element.9) | data formatting | bytes 524288

commit v2 on v1

--- a/solution.py
+++ b/solution.py
@@ -14,7 +14,7 @@
 NT = ((1,), (1,))
 TN = ((0,), (0,))
 LANES = 128
-CHUNKS = 2
+CHUNKS = 4
 
 
 def dot(left, right, dims=NN):
@@ -39,10 +39,10 @@
     enc_w,
     vec,
     init,
-    mesh_w,
+    mesh_hbm,
     sends,
     sources,
-    proc_w,
+    proc_hbm,
     cot,
     mesh_out,
     grid_grad,
@@ -66,6 +66,9 @@
     act_slope,
     joined,
     far_part,
+    mesh_w,
+    proc_w,
+    load_sem,
     far_grad,
     piece,
     last_part,
@@ -77,8 +80,8 @@
     world = sects * nodes
     zero = lax.div(sect, sects)
     line = sect * nodes + node
-    grid_rows, fanout = length.shape
-    block, degree = sources.shape
+    fanout, grid_rows = length.shape
+    degree, block = sources.shape
     width = feat.shape[1]
     whole = block * sects
     cap = msg_out.shape[2]
@@ -88,6 +91,13 @@
     layers = proc_w.shape[0]
     fan = halo_out.shape[2]
     halo = world * fan
+
+    loads = [
+        pltpu.make_async_copy(mesh_hbm, mesh_w, load_sem.at[0]),
+        pltpu.make_async_copy(proc_hbm, proc_w, load_sem.at[1]),
+    ]
+    for load in loads:
+        load.start()
 
     barrier = pltpu.get_barrier_semaphore()
 
@@ -168,7 +178,10 @@
     dst_out[...] = table.reshape(nodes, 1, LANES)
 
     pre = dot(feat[...], enc_w[...])
-    acts = [pre + length[:, k : k + 1] * vec[...] for k in range(fanout)]
+    acts = []
+    for k in range(fanout):
+        column = jnp.broadcast_to(length[k : k + 1, :], (8, grid_rows)).T[:, 0:1]
+        acts.append(pre + column * vec[...])
     sigs = [jax.nn.sigmoid(act) for act in acts]
     message = jnp.concatenate(
         [(act * sig).astype(BF16) for act, sig in zip(acts, sigs)], axis=0
@@ -187,10 +200,16 @@
         act_slope[k] = slope_of(acts[k], sigs[k])
 
     for k in range(degree):
-        edge_pick[k * block : (k + 1) * block, :] = (
-            iota((block, block + halo), 1) == sources[:, k : k + 1]
+        edge_pick[:, k * block : (k + 1) * block] = (
+            iota((block + halo, block), 0) == sources[k : k + 1, :]
         ).astype(BF16)
-    halo_pick = (iota((block, halo), 0) == sends[...]).astype(BF16)
+    order = iota((nodes, halo), 1)
+    spread = (lax.rem(lax.div(order, fan), nodes) == iota((nodes, halo), 0)).astype(BF16)
+    order = iota((sects * fan, halo), 1)
+    mine = lax.div(order, fan * nodes) * fan + lax.rem(order, fan) == iota(order.shape, 0)
+    wide = dot(sends[...].astype(F32).astype(BF16), spread)
+    sent = jnp.sum(jnp.where(mine, wide, 0.0), axis=0, keepdims=True).astype(jnp.int32)
+    halo_pick = (iota((block, halo), 0) == sent).astype(BF16)
 
     landed(dst_in, nodes - 1, recv_sem.at[at_dst])
     got = dst_in[...].reshape(nodes, LANES)
@@ -203,7 +222,8 @@
     scat[...] = (iota((whole, slots), 0) == got_row).astype(BF16)
 
     mesh_pre = jnp.zeros((block, width), F32)
-    own_part = []
+    for load in loads:
+        load.wait()
     for c in range(chunks):
         landed(msg_in.at[c], nodes - 1, recv_sem.at[at_msg + c])
         agg = dot(scat[...], msg_in[c].reshape(slots, part))
@@ -227,7 +247,7 @@
         halo_out[layer] = out.reshape(world, fan, width)
         over_all(halo_out.at[layer], halo_in.at[layer], at_halo + layer)
         halo_in[layer, line] = halo_out[layer, line]
-        near = dot(edge_pick[:, :block], state).astype(BF16)
+        near = dot(edge_pick[:block, :], state, TN).astype(BF16)
         piece[2] = dot(state, proc_w[layer, 1])
         joined[layer] = dot(near, proc_w[layer, 0])
         piece[1] = dot(state, proc_w[layer, 2])
@@ -235,7 +255,7 @@
             prev = joined[layer - 1]
             joined[layer - 1] = slope_of(prev, jax.nn.sigmoid(prev))
         landed(halo_in.at[layer], world - 1, recv_sem.at[at_halo + layer])
-        far = dot(edge_pick[:, block:], halo_in[layer].reshape(halo, width)).astype(BF16)
+        far = dot(edge_pick[block:, :], halo_in[layer].reshape(halo, width), TN).astype(BF16)
         far_part[...] = dot(far, proc_w[layer, 0])
         agg = jnp.zeros((block, width), F32)
         to_dst = piece[zero + 2]
@@ -275,13 +295,13 @@
             grad_dst = grad_dst + grad_joined
             far_grad[rows, :] = grad_joined.astype(BF16)
         grad_dst = grad_dst.astype(BF16)
-        out = dot(edge_pick[:, block:], far_grad[...], TN).astype(BF16)
+        out = dot(edge_pick[block:, :], far_grad[...]).astype(BF16)
         back_out[layer] = out.reshape(world, fan, width)
         over_all(back_out.at[layer], back_in.at[layer], at_back + layer)
         back_in[layer, line] = back_out[layer, line]
         piece[0] = dot(grad_mixed, proc_w[layer, 2], NT)
         piece[1] = dot(grad_dst, proc_w[layer, 1], NT)
-        piece[2] = dot(edge_pick[:, :block], far_grad[...], TN)
+        piece[2] = dot(edge_pick[:block, :], far_grad[...])
         landed(back_in.at[layer], world - 1, recv_sem.at[at_back + layer])
         piece[3] = dot(halo_pick, back_in[layer].reshape(halo, width))
         grad_src = (piece[zero + 2] + piece[zero + 3]).astype(BF16)
@@ -326,6 +346,11 @@
     for layer in range(layers):
         landed(halo_out.at[layer], world - 1, send_sem.at[at_halo + layer])
         landed(back_out.at[layer], world - 1, send_sem.at[at_back + layer])
+
+
+def finish(state, grad, mesh_out, grid_grad):
+    mesh_out[...] = state[...]
+    grid_grad[...] = grad[...]
 
 
 def body(
@@ -358,13 +383,15 @@
     whole = block * sects
     count = 1 + 4 * chunks + 2 * layers
     vmem = pl.BlockSpec(memory_space=pltpu.VMEM)
+    hbm = pl.BlockSpec(memory_space=pl.ANY)
+    out_shape = (
+        jax.ShapeDtypeStruct((block, width), BF16),
+        jax.ShapeDtypeStruct((grid_rows, width), BF16),
+    )
     out = pl.pallas_call(
         functools.partial(fused, sects, nodes),
-        out_shape=(
-            jax.ShapeDtypeStruct((block, width), BF16),
-            jax.ShapeDtypeStruct((grid_rows, width), BF16),
-        ),
-        in_specs=[vmem] * 12,
+        out_shape=out_shape,
+        in_specs=[vmem] * 7 + [hbm, vmem, vmem, hbm, vmem],
         out_specs=(vmem, vmem),
         scratch_shapes=[
             pltpu.VMEM((nodes, 1, LANES), F32),
@@ -383,10 +410,13 @@
             pltpu.VMEM((chunks, nodes, cap, part), BF16),
             pltpu.VMEM((slots, fanout * grid_rows), BF16),
             pltpu.VMEM((whole, slots), BF16),
-            pltpu.VMEM((degree * block, block + world * fan), BF16),
+            pltpu.VMEM((block + world * fan, degree * block), BF16),
             pltpu.VMEM((fanout, grid_rows, width), F32),
             pltpu.VMEM((layers, degree * block, width), F32),
             pltpu.VMEM((degree * block, width), F32),
+            pltpu.VMEM(mesh_weight.shape, BF16),
+            pltpu.VMEM(proc_weight.shape, BF16),
+            pltpu.SemaphoreType.DMA((2,)),
             pltpu.VMEM((degree * block, width), BF16),
             pltpu.VMEM((5, block, width), F32),
             pltpu.VMEM((chunks, grid_rows, width), F32),
@@ -399,18 +429,25 @@
         name="grid_mesh",
     )(
         grid_feat,
-        edge_len,
+        edge_len.T,
         g2m_owner.T,
         g2m_dst.T,
         enc_weight,
         enc_vec.reshape(1, width),
         mesh_init[0],
         mesh_weight,
-        halo_send.reshape(1, world * fan),
-        mesh_src[0],
+        halo_send[0, 0].transpose(0, 2, 1).reshape(sects * fan, nodes),
+        mesh_src[0].T,
         proc_weight,
         cot[0],
     )
+    out = pl.pallas_call(
+        finish,
+        out_shape=out_shape,
+        in_specs=[vmem] * 2,
+        out_specs=(vmem, vmem),
+        name="finish",
+    )(*out)
     return (out[0][None], out[1])
 
 

time: 164 us -> 155 us (0.945)
  local copies, waits for them, and re-layouts: 7.63 us -> 0 us
  Pallas kernels: 154 us -> 152 us
    unnamed x5 -> x0, local copies, waits for them, and re-layouts: 6.92 us -> none
    pallas_call x1 -> x2, Pallas kernels: 154 us -> 152 us  [the longest x1 150 us: body(): pl.pallas_call(functools.partial(fused, sects, nodes), out_shape=out_shap...]
where the time goes in v2:
time: 155 us; the launch traced here: 153 us
  Pallas kernels  152 us (98%)
    pallas_call x1, Pallas kernels, body(): pl.pallas_call(functools.partial(fused, sects, nodes), out_shape=out_shap...  150 us

profile of v2, /device:TPU:8, one launch (start us, length us, event | category | flops | bytes accessed | tf_op | source)
XLA Modules:
  0.0 152.8 jit_solution(13829384444122500898)
XLA Ops:
  0.6 150.4 %grid_mesh.1 = (bf16[128,512]{1,0:T(8,128)(2,1)}, bf16[256,512]{1,0:T(8,128)(2,1)}) custom-call(bf16[256,512]{1,0:T(8,128)(2,1)} %feat.1, f32[2,256]{1,0:T(2,128)} %bitcast.19, s32[2,256]{1,0:T(2,128)} %bitcast.20, s32[2,256]{1,0:T(2,128)} %bitcast.21, bf16[512,512]{1,0:T(8,128)(2,1)} %enc_w.1, f32[1,512]{1,0:T(1,128)} %bitcast.22, ...), custom_call_target="tpu_custom_call" | custom-call | tf_op jit(solution)/shard_map/grid_mesh/pallas_call | solution.py:391
  151.0 1.8 %finish.1 = (bf16[128,512]{1,0:T(8,128)(2,1)}, bf16[256,512]{1,0:T(8,128)(2,1)}) custom-call(bf16[128,512]{1,0:T(8,128)(2,1)} %get-tuple-element.6.state, bf16[256,512]{1,0:T(8,128)(2,1)} %get-tuple-element.7.grad), custom_call_target="tpu_custom_call" | custom-call | tf_op jit(solution)/shard_map/finish/pallas_call | solution.py:444

commit v3 on v2

--- a/solution.py
+++ b/solution.py
@@ -32,11 +32,11 @@
 def fused(
     sects,
     nodes,
-    feat,
+    feat_hbm,
     length,
     owner,
     dest,
-    enc_w,
+    enc_hbm,
     vec,
     init,
     mesh_hbm,
@@ -63,9 +63,12 @@
     pick,
     scat,
     edge_pick,
+    halo_pick,
     act_slope,
     joined,
     far_part,
+    feat,
+    enc_w,
     mesh_w,
     proc_w,
     load_sem,
@@ -91,10 +94,13 @@
     layers = proc_w.shape[0]
     fan = halo_out.shape[2]
     halo = world * fan
+    span = nodes * fan
 
     loads = [
-        pltpu.make_async_copy(mesh_hbm, mesh_w, load_sem.at[0]),
-        pltpu.make_async_copy(proc_hbm, proc_w, load_sem.at[1]),
+        pltpu.make_async_copy(feat_hbm, feat, load_sem.at[0]),
+        pltpu.make_async_copy(enc_hbm, enc_w, load_sem.at[1]),
+        pltpu.make_async_copy(mesh_hbm, mesh_w, load_sem.at[2]),
+        pltpu.make_async_copy(proc_hbm, proc_w, load_sem.at[3]),
     ]
     for load in loads:
         load.start()
@@ -132,18 +138,13 @@
 
         lax.fori_loop(1, nodes, step, 0, unroll=9)
 
-    def over_all(src, dst, at):
+    def over_sect(src, dst, at, peer_sect, first):
         def step(off, carry):
-            peer = lax.rem(line + off, world)
-            push(
-                src.at[peer],
-                dst.at[line],
-                at,
-                (lax.div(peer, nodes), lax.rem(peer, nodes)),
-            )
+            peer = lax.rem(node + off, nodes)
+            push(src.at[peer_sect * nodes + peer], dst.at[line], at, (peer_sect, peer))
             return carry
 
-        lax.fori_loop(1, world, step, 0, unroll=15)
+        lax.fori_loop(int(first), nodes, step, 0, unroll=9 if first else 8)
 
     def landed(ref, count, sem):
         some = ref.at[pl.ds(0, count)]
@@ -159,10 +160,9 @@
 
     upper = (iota((grid_rows, grid_rows), 0) < iota((grid_rows, grid_rows), 1)).astype(BF16)
     used = jnp.zeros((nodes, 1), F32)
-    table = jnp.zeros((nodes, LANES), F32)
+    hots, ranks, columns = [], [], []
     for k in range(fanout):
         own_row = owner[k : k + 1, :]
-        dst_row = dest[k : k + 1, :]
         hot = (iota((nodes, grid_rows), 0) == own_row).astype(F32)
         before = dot(hot.astype(BF16), upper) + used
         rank = jnp.sum(hot * before, axis=0, keepdims=True).astype(jnp.int32)
@@ -171,33 +171,38 @@
         pick[:, k * grid_rows : (k + 1) * grid_rows] = (
             iota((slots, grid_rows), 0) == place
         ).astype(BF16)
-        level = (iota((LANES, grid_rows), 0) == rank).astype(BF16)
-        high = (hot * (dst_row >> 4).astype(F32)).astype(BF16)
-        low = (hot * ((dst_row & 15) + 1).astype(F32)).astype(BF16)
-        table = table + 16.0 * dot(high, level, NT) + dot(low, level, NT)
-    dst_out[...] = table.reshape(nodes, 1, LANES)
-
-    pre = dot(feat[...], enc_w[...])
-    acts = []
-    for k in range(fanout):
-        column = jnp.broadcast_to(length[k : k + 1, :], (8, grid_rows)).T[:, 0:1]
-        acts.append(pre + column * vec[...])
-    sigs = [jax.nn.sigmoid(act) for act in acts]
-    message = jnp.concatenate(
-        [(act * sig).astype(BF16) for act, sig in zip(acts, sigs)], axis=0
-    )
-
-    pl.semaphore_wait(barrier, nodes + sects - 2)
-    over_nodes(dst_out, dst_in, at_dst)
-    dst_in[node] = dst_out[node]
+        hots.append(hot)
+        ranks.append(rank)
+        columns.append(jnp.broadcast_to(length[k : k + 1, :], (8, grid_rows)).T[:, 0:1])
+
+    for load in loads[:2]:
+        load.wait()
     for c in range(chunks):
         cols = slice(c * part, (c + 1) * part)
-        msg_out[c] = dot(pick[...], message[:, cols]).astype(BF16).reshape(nodes, cap, part)
+        pre = dot(feat[...], enc_w[:, cols])
+        message = []
+        for k in range(fanout):
+            act = pre + columns[k] * vec[:, cols]
+            sig = jax.nn.sigmoid(act)
+            message.append((act * sig).astype(BF16))
+            act_slope[k, :, cols] = slope_of(act, sig)
+        message = jnp.concatenate(message, axis=0)
+        msg_out[c] = dot(pick[...], message).astype(BF16).reshape(nodes, cap, part)
+        if c == 0:
+            pl.semaphore_wait(barrier, nodes + sects - 2)
         over_nodes(msg_out.at[c], msg_in.at[c], at_msg + c)
         msg_in[c, node] = msg_out[c, node]
-
-    for k in range(fanout):
-        act_slope[k] = slope_of(acts[k], sigs[k])
+        if c == 0:
+            table = jnp.zeros((nodes, LANES), F32)
+            for k in range(fanout):
+                dst_row = dest[k : k + 1, :]
+                level = (iota((LANES, grid_rows), 0) == ranks[k]).astype(BF16)
+                high = (hots[k] * (dst_row >> 4).astype(F32)).astype(BF16)
+                low = (hots[k] * ((dst_row & 15) + 1).astype(F32)).astype(BF16)
+                table = table + 16.0 * dot(high, level, NT) + dot(low, level, NT)
+            dst_out[...] = table.reshape(nodes, 1, LANES)
+            over_nodes(dst_out, dst_in, at_dst)
+            dst_in[node] = dst_out[node]
 
     for k in range(degree):
         edge_pick[:, k * block : (k + 1) * block] = (
@@ -209,7 +214,7 @@
     mine = lax.div(order, fan * nodes) * fan + lax.rem(order, fan) == iota(order.shape, 0)
     wide = dot(sends[...].astype(F32).astype(BF16), spread)
     sent = jnp.sum(jnp.where(mine, wide, 0.0), axis=0, keepdims=True).astype(jnp.int32)
-    halo_pick = (iota((block, halo), 0) == sent).astype(BF16)
+    halo_pick[...] = (iota((block, halo), 0) == sent).astype(BF16)
 
     landed(dst_in, nodes - 1, recv_sem.at[at_dst])
     got = dst_in[...].reshape(nodes, LANES)
@@ -222,7 +227,7 @@
     scat[...] = (iota((whole, slots), 0) == got_row).astype(BF16)
 
     mesh_pre = jnp.zeros((block, width), F32)
-    for load in loads:
+    for load in loads[2:]:
         load.wait()
     for c in range(chunks):
         landed(msg_in.at[c], nodes - 1, recv_sem.at[at_msg + c])
@@ -243,9 +248,12 @@
 
     saved = []
     for layer in range(layers):
-        out = dot(halo_pick, state, TN).astype(BF16)
-        halo_out[layer] = out.reshape(world, fan, width)
-        over_all(halo_out.at[layer], halo_in.at[layer], at_halo + layer)
+        for off in range(sects):
+            peer = lax.rem(sect + off, sects)
+            cols = pl.ds(pl.multiple_of(peer * span, span), span)
+            out = dot(halo_pick[:, cols], state, TN).astype(BF16)
+            halo_out[layer, pl.ds(peer * nodes, nodes)] = out.reshape(nodes, fan, width)
+            over_sect(halo_out.at[layer], halo_in.at[layer], at_halo + layer, peer, off == 0)
         halo_in[layer, line] = halo_out[layer, line]
         near = dot(edge_pick[:block, :], state, TN).astype(BF16)
         piece[2] = dot(state, proc_w[layer, 1])
@@ -255,15 +263,19 @@
             prev = joined[layer - 1]
             joined[layer - 1] = slope_of(prev, jax.nn.sigmoid(prev))
         landed(halo_in.at[layer], world - 1, recv_sem.at[at_halo + layer])
-        far = dot(edge_pick[block:, :], halo_in[layer].reshape(halo, width), TN).astype(BF16)
-        far_part[...] = dot(far, proc_w[layer, 0])
+        incoming = halo_in[layer].reshape(halo, width)
         agg = jnp.zeros((block, width), F32)
         to_dst = piece[zero + 2]
         for k in range(degree):
+            if k % (degree // 2) == 0:
+                some = slice(k * block, (k + degree // 2) * block)
+                far = dot(edge_pick[block:, some], incoming, TN).astype(BF16)
+                far_part[some, :] = dot(far, proc_w[layer, 0])
             rows = slice(k * block, (k + 1) * block)
             full = joined[zero + layer, rows, :] + far_part[rows, :] + to_dst
-            joined[layer, rows, :] = full
-            agg = agg + full * jax.nn.sigmoid(full)
+            gate = jax.nn.sigmoid(full)
+            joined[layer, rows, :] = full if layer < layers - 1 else slope_of(full, gate)
+            agg = agg + full * gate
         agg = agg.astype(BF16)
         piece[0] = dot(agg, proc_w[layer, 3])
         mixed = piece[zero + 1] + piece[zero]
@@ -274,8 +286,6 @@
         saved.append((normed, scale, slope_of(normed, sig)))
         state = (state.astype(F32) + normed * sig).astype(BF16)
     mesh_out[...] = state
-    last = joined[layers - 1]
-    joined[layers - 1] = slope_of(last, jax.nn.sigmoid(last))
 
     grad = cot[...].astype(F32)
     for layer in reversed(range(layers)):
@@ -295,15 +305,18 @@
             grad_dst = grad_dst + grad_joined
             far_grad[rows, :] = grad_joined.astype(BF16)
         grad_dst = grad_dst.astype(BF16)
-        out = dot(edge_pick[block:, :], far_grad[...]).astype(BF16)
-        back_out[layer] = out.reshape(world, fan, width)
-        over_all(back_out.at[layer], back_in.at[layer], at_back + layer)
+        for off in range(sects):
+            peer = lax.rem(sect + off, sects)
+            rows = pl.ds(pl.multiple_of(block + peer * span, span), span)
+            out = dot(edge_pick[rows, :], far_grad[...]).astype(BF16)
+            back_out[layer, pl.ds(peer * nodes, nodes)] = out.reshape(nodes, fan, width)
+            over_sect(back_out.at[layer], back_in.at[layer], at_back + layer, peer, off == 0)
         back_in[layer, line] = back_out[layer, line]
         piece[0] = dot(grad_mixed, proc_w[layer, 2], NT)
         piece[1] = dot(grad_dst, proc_w[layer, 1], NT)
         piece[2] = dot(edge_pick[:block, :], far_grad[...])
         landed(back_in.at[layer], world - 1, recv_sem.at[at_back + layer])
-        piece[3] = dot(halo_pick, back_in[layer].reshape(halo, width))
+        piece[3] = dot(halo_pick[...], back_in[layer].reshape(halo, width))
         grad_src = (piece[zero + 2] + piece[zero + 3]).astype(BF16)
         piece[4] = dot(grad_src, proc_w[layer, 0], NT)
         grad = grad + piece[zero] + piece[zero + 1] + piece[zero + 4]
@@ -391,7 +404,7 @@
     out = pl.pallas_call(
         functools.partial(fused, sects, nodes),
         out_shape=out_shape,
-        in_specs=[vmem] * 7 + [hbm, vmem, vmem, hbm, vmem],
+        in_specs=[hbm, vmem, vmem, vmem, hbm, vmem, vmem, hbm, vmem, vmem, hbm, vmem],
         out_specs=(vmem, vmem),
         scratch_shapes=[
             pltpu.VMEM((nodes, 1, LANES), F32),
@@ -411,12 +424,15 @@
             pltpu.VMEM((slots, fanout * grid_rows), BF16),
             pltpu.VMEM((whole, slots), BF16),
             pltpu.VMEM((block + world * fan, degree * block), BF16),
+            pltpu.VMEM((block, world * fan), BF16),
             pltpu.VMEM((fanout, grid_rows, width), F32),
             pltpu.VMEM((layers, degree * block, width), F32),
             pltpu.VMEM((degree * block, width), F32),
+            pltpu.VMEM(grid_feat.shape, BF16),
+            pltpu.VMEM(enc_weight.shape, BF16),
             pltpu.VMEM(mesh_weight.shape, BF16),
             pltpu.VMEM(proc_weight.shape, BF16),
-            pltpu.SemaphoreType.DMA((2,)),
+            pltpu.SemaphoreType.DMA((4,)),
             pltpu.VMEM((degree * block, width), BF16),
             pltpu.VMEM((5, block, width), F32),
             pltpu.VMEM((chunks, grid_rows, width), F32),

time: 155 us -> 152 us (0.981)
  Pallas kernels: 152 us -> 150 us
    pallas_call x1, Pallas kernels: 150 us -> 148 us  [body(): pl.pallas_call(functools.partial(fused, sects, nodes), out_shape=out_shap...]
where the time goes in v3:
time: 152 us; the launch traced here: 150 us
  Pallas kernels  150 us (99%)
    pallas_call x1, Pallas kernels, body(): pl.pallas_call(functools.partial(fused, sects, nodes), out_shape=out_shap...  148 us

profile of v3, /device:TPU:8, one launch (start us, length us, event | category | flops | bytes accessed | tf_op | source)
XLA Modules:
  0.0 150.5 jit_solution(10757161328765321310)
XLA Ops:
  0.6 148.0 %grid_mesh.1 = (bf16[128,512]{1,0:T(8,128)(2,1)}, bf16[256,512]{1,0:T(8,128)(2,1)}) custom-call(bf16[256,512]{1,0:T(8,128)(2,1)} %feat_hbm.1, f32[2,256]{1,0:T(2,128)} %bitcast.19, s32[2,256]{1,0:T(2,128)} %bitcast.20, s32[2,256]{1,0:T(2,128)} %bitcast.21, bf16[512,512]{1,0:T(8,128)(2,1)} %enc_hbm.1, f32[1,512]{1,0:T(1,128)} %bitcast.22, ...), custom_call_target="tpu_custom_call" | custom-call | tf_op jit(solution)/shard_map/grid_mesh/pallas_call | solution.py:404
  148.7 1.8 %finish.1 = (bf16[128,512]{1,0:T(8,128)(2,1)}, bf16[256,512]{1,0:T(8,128)(2,1)}) custom-call(bf16[128,512]{1,0:T(8,128)(2,1)} %get-tuple-element.6.state, bf16[256,512]{1,0:T(8,128)(2,1)} %get-tuple-element.7.grad), custom_call_target="tpu_custom_call" | custom-call | tf_op jit(solution)/shard_map/finish/pallas_call | solution.py:460

commit v4 on v3

--- a/solution.py
+++ b/solution.py
@@ -154,7 +154,7 @@
     at_msg = 1
     at_part = at_msg + chunks
     at_halo = at_part + chunks
-    at_back = at_halo + layers
+    at_back = at_halo + layers * sects
     at_gath = at_back + layers
     at_slot = at_gath + chunks
 
@@ -253,7 +253,7 @@
             cols = pl.ds(pl.multiple_of(peer * span, span), span)
             out = dot(halo_pick[:, cols], state, TN).astype(BF16)
             halo_out[layer, pl.ds(peer * nodes, nodes)] = out.reshape(nodes, fan, width)
-            over_sect(halo_out.at[layer], halo_in.at[layer], at_halo + layer, peer, off == 0)
+            over_sect(halo_out.at[layer], halo_in.at[layer], at_halo + layer * sects + off, peer, off == 0)
         halo_in[layer, line] = halo_out[layer, line]
         near = dot(edge_pick[:block, :], state, TN).astype(BF16)
         piece[2] = dot(state, proc_w[layer, 1])
@@ -262,15 +262,25 @@
         if layer > 0:
             prev = joined[layer - 1]
             joined[layer - 1] = slope_of(prev, jax.nn.sigmoid(prev))
-        landed(halo_in.at[layer], world - 1, recv_sem.at[at_halo + layer])
-        incoming = halo_in[layer].reshape(halo, width)
+        every = pl.ds(pl.multiple_of(zero * block, block), degree * block)
+        for off in range(sects):
+            peer = lax.rem(sect + sects - off, sects)
+            landed(
+                halo_in.at[layer, pl.ds(peer * nodes, nodes)],
+                nodes - int(off == 0),
+                recv_sem.at[at_halo + layer * sects + off],
+            )
+            rows = pl.ds(pl.multiple_of(block + peer * span, span), span)
+            incoming = halo_in[layer, pl.ds(peer * nodes, nodes)].reshape(span, width)
+            found = dot(edge_pick[rows, :], incoming, TN)
+            far_part[...] = found if off == 0 else far_part[every, :] + found
+        far_rows = far_part[every, :].astype(BF16)
         agg = jnp.zeros((block, width), F32)
         to_dst = piece[zero + 2]
         for k in range(degree):
             if k % (degree // 2) == 0:
                 some = slice(k * block, (k + degree // 2) * block)
-                far = dot(edge_pick[block:, some], incoming, TN).astype(BF16)
-                far_part[some, :] = dot(far, proc_w[layer, 0])
+                far_part[some, :] = dot(far_rows[some, :], proc_w[layer, 0])
             rows = slice(k * block, (k + 1) * block)
             full = joined[zero + layer, rows, :] + far_part[rows, :] + to_dst
             gate = jax.nn.sigmoid(full)
@@ -357,7 +367,13 @@
         landed(gath_in.at[c], sects - 1, send_sem.at[at_gath + c])
         landed(slot_out.at[c], nodes - 1, send_sem.at[at_slot + c])
     for layer in range(layers):
-        landed(halo_out.at[layer], world - 1, send_sem.at[at_halo + layer])
+        for off in range(sects):
+            peer = lax.rem(sect + off, sects)
+            landed(
+                halo_out.at[layer, pl.ds(peer * nodes, nodes)],
+                nodes - int(off == 0),
+                send_sem.at[at_halo + layer * sects + off],
+            )
         landed(back_out.at[layer], world - 1, send_sem.at[at_back + layer])
 
 
@@ -394,7 +410,7 @@
     chunks = CHUNKS
     part = width // chunks
     whole = block * sects
-    count = 1 + 4 * chunks + 2 * layers
+    count = 1 + 4 * chunks + (1 + sects) * layers
     vmem = pl.BlockSpec(memory_space=pltpu.VMEM)
     hbm = pl.BlockSpec(memory_space=pl.ANY)
     out_shape = (

time: 152 us -> 153 us (level)
  no operation moved by 1% of the time
where the time goes in v4:
time: 153 us; the launch traced here: 151 us
  Pallas kernels  151 us (99%)
    pallas_call x1, Pallas kernels, body(): pl.pallas_call(functools.partial(fused, sects, nodes), out_shape=out_shap...  149 us

profile of v4, /device:TPU:8, one launch (start us, length us, event | category | flops | bytes accessed | tf_op | source)
XLA Modules:
  0.0 151.2 jit_solution(1216537281649494454)
XLA Ops:
  0.6 148.8 %grid_mesh.1 = (bf16[128,512]{1,0:T(8,128)(2,1)}, bf16[256,512]{1,0:T(8,128)(2,1)}) custom-call(bf16[256,512]{1,0:T(8,128)(2,1)} %feat_hbm.1, f32[2,256]{1,0:T(2,128)} %bitcast.19, s32[2,256]{1,0:T(2,128)} %bitcast.20, s32[2,256]{1,0:T(2,128)} %bitcast.21, bf16[512,512]{1,0:T(8,128)(2,1)} %enc_hbm.1, f32[1,512]{1,0:T(1,128)} %bitcast.22, ...), custom_call_target="tpu_custom_call" | custom-call | tf_op jit(solution)/shard_map/grid_mesh/pallas_call | solution.py:420
  149.4 1.8 %finish.1 = (bf16[128,512]{1,0:T(8,128)(2,1)}, bf16[256,512]{1,0:T(8,128)(2,1)}) custom-call(bf16[128,512]{1,0:T(8,128)(2,1)} %get-tuple-element.6.state, bf16[256,512]{1,0:T(8,128)(2,1)} %get-tuple-element.7.grad), custom_call_target="tpu_custom_call" | custom-call | tf_op jit(solution)/shard_map/finish/pallas_call | solution.py:476
